TPU v7x, 32 devices: a whole 2x2x4 slice. The times are simulated.
32 devices in a mesh: expert: 32 (over z, y, x, core), tensor: 1.
Axes of the slice: x: 2, y: 2, z: 4, core: 2. Of those that a mesh axis runs over, the one named last changes fastest.
Arguments:
- hidden_rows: bfloat16 [2, 512, 3584], P(None, 'expert', 'tensor'), may hold values from -6 to 6
- draft_len: int32 [2, 128], P(None, 'expert'), may hold values from 1 to 4, 320 in all within a row
- expert_ids: int32 [2, 512, 8], P(None, 'expert'), may hold values from 0 to 27, all different within a row; in each aligned block of 16 rows (0 to 15, 16 to 31, ..., all dimensions but the last counted through in order) at most 6 rows name the same one
- replica: int32 [2, 512, 8], P(None, 'expert'), may hold values from 0 to 1
- route_gain: float32 [2, 512, 8], P(None, 'expert'), may hold values from 0.03 to 0.5
- slot_up: bfloat16 [32, 3584, 1024], P('expert', None, 'tensor'), may hold values from -0.09375 to 0.09375
- slot_down: bfloat16 [32, 1024, 3584], P('expert', 'tensor'), may hold values from -0.1875 to 0.1875
- shared_up: bfloat16 [3584, 1024], P(None, 'tensor'), may hold values from -0.09375 to 0.09375
- shared_down: bfloat16 [1024, 3584], P('tensor'), may hold values from -0.1875 to 0.1875
Outputs:
- mixed: bfloat16 [2, 512, 3584], P(None, 'expert', 'tensor')
Inputs may be any that keep to these rules, and one draw needn't show every extreme that they name: `expert_ids`: in each step, the 16 row places of one index of expert (live or not) name any one expert at most 6 times. Only the first 4 experts have a replica slot; for the other experts the value has no effect. `draft_len`: in each step the lengths of all 128 requests sum to 320.
All inputs are finite; a program needn't handle non-finite values. No bound on the sum of `draft_len` on one device may be relied on, other than what follows from the above.
Results may differ from a plain program's by a relative error of at most 0.019.
Values may be sent and summed in bfloat16 or wider, within the bound.
A program may use at most 192 MiB of HBM per device.

v0:
```python
import jax
import jax.numpy as jnp
from jax import lax
from jax.sharding import PartitionSpec as P


def route_plan(lengths, chosen, second, gains, slot_count, capacity):
    row_count, top_count = chosen.shape
    span_rows = row_count // lengths.shape[0]
    positions = jnp.arange(row_count, dtype=jnp.int32)
    limit = jnp.repeat(lengths, span_rows, total_repeat_length=row_count)
    live_mask = positions % span_rows < limit
    replicas = slot_count // 8
    experts_all = slot_count - replicas
    slot_index = jnp.where(
        (chosen < replicas) & (second == 1), chosen + experts_all, chosen
    ).reshape(-1)
    valid = jnp.broadcast_to(live_mask[:, None], chosen.shape).reshape(-1)
    onehot = (
        (slot_index[:, None] == jnp.arange(slot_count, dtype=jnp.int32)[None, :]) & valid[:, None]
    ).astype(jnp.int32)
    earlier = jnp.cumsum(onehot, axis=0) - onehot
    order_rank = jnp.sum(earlier * onehot, axis=1)
    target = jnp.where(valid, slot_index * capacity + order_rank, -1)
    buffer_ids = jnp.arange(slot_count * capacity, dtype=jnp.int32)
    picker = jnp.any(
        target.reshape(row_count, top_count)[None, :, :] == buffer_ids[:, None, None], axis=2
    ).astype(jnp.bfloat16)
    weights = (gains * live_mask[:, None].astype(jnp.float32)).reshape(-1)
    return (live_mask, target, picker, weights)


def shards(
    hidden_rows,
    draft_len,
    expert_ids,
    replica,
    route_gain,
    slot_up,
    slot_down,
    shared_up,
    shared_down,
):
    slot_count = lax.axis_size("expert")
    step_count, row_count, _ = hidden_rows.shape
    top_count = expert_ids.shape[2]
    capacity = row_count * top_count // (slot_count - slot_count // 8) + 2
    gathered = lax.all_gather(hidden_rows, "tensor", axis=2, tiled=True)
    width_full = gathered.shape[2]
    plans = [
        route_plan(
            draft_len[index],
            expert_ids[index],
            replica[index],
            route_gain[index],
            slot_count,
            capacity,
        )
        for index in range(step_count)
    ]
    outgoing = []
    for index in range(step_count):
        source = gathered[index]
        packed = jnp.dot(plans[index][2], source, preferred_element_type=jnp.float32).astype(
            jnp.bfloat16
        )
        outgoing.append(packed.reshape(slot_count, capacity, source.shape[1]))
    groups = [[index] for index in range(step_count)]
    returned = [None] * step_count
    for step_group in groups:
        batch = jnp.concatenate([outgoing[index] for index in step_group], axis=1)
        received = lax.all_to_all(batch, "expert", split_axis=0, concat_axis=0, tiled=True)
        flat_rows = received.reshape(-1, width_full)
        hidden = jax.nn.silu(
            jnp.dot(flat_rows, slot_up[0], preferred_element_type=jnp.float32)
        ).astype(jnp.bfloat16)
        partial_value = jnp.dot(hidden, slot_down[0], preferred_element_type=jnp.float32).astype(
            jnp.bfloat16
        )
        partial_value = partial_value.reshape(received.shape[0], -1, width_full)
        answer = lax.all_to_all(partial_value, "expert", split_axis=0, concat_axis=0, tiled=True)
        out_width = answer.shape[2]
        for place, index in enumerate(step_group):
            returned[index] = answer.reshape(-1, out_width)
    routed_terms = []
    shared_terms = []
    for index in range(step_count):
        live_mask, target, picker, weights = plans[index]
        fetched = jnp.take(returned[index], jnp.maximum(target, 0), axis=0).astype(jnp.float32)
        routed = jnp.sum(
            (fetched * weights[:, None]).reshape(row_count, top_count, fetched.shape[1]), axis=1
        )
        shared_act = jax.nn.silu(
            jnp.dot(gathered[index], shared_up, preferred_element_type=jnp.float32)
        ).astype(jnp.bfloat16)
        shared_out = jnp.dot(shared_act, shared_down, preferred_element_type=jnp.float32)
        routed_terms.append(routed)
        shared_terms.append(shared_out)
    live_all = jnp.stack([plans[index][0] for index in range(step_count)]).astype(jnp.float32)[
        :, :, None
    ]
    terms = (jnp.stack(routed_terms) + jnp.stack(shared_terms)) * live_all
    summed = lax.psum_scatter(terms.astype(jnp.bfloat16), "tensor", scatter_dimension=2, tiled=True)
    return summed


def solution(mesh):
    return jax.shard_map(
        shards,
        mesh=mesh,
        in_specs=(
            P(None, "expert", "tensor"),
            P(None, "expert"),
            P(None, "expert", None),
            P(None, "expert", None),
            P(None, "expert", None),
            P("expert", None, "tensor"),
            P("expert", "tensor", None),
            P(None, "tensor"),
            P("tensor", None),
        ),
        out_specs=P(None, "expert", "tensor"),
        check_vma=False,
    )
```

profile of v0, /device:TPU:1, one launch (start us, length us, event | category | flops | bytes accessed | tf_op | source)
XLA Modules:
  0.0 207.0 jit_solution(15323066669139499485)
XLA Ops:
  1.8 0.8 slice_bitcast_fusion.1
  5.5 1.5 convolution_convert_fusion
  6.9 1.5 reshape.196
  8.4 7.1 %all-to-all-start.2 = ((bf16[32,6,3584]{2,1,0:T(8,128)(2,1)}), bf16[32,6,3584]{2,1,0:T(8,128)(2,1)S(1)}, u32[]{:S(2)}, u32[]{:S(2)}) async-start(bf16[32,6,3584]{2,1,0:T(8,128)(2,1)} %reshape.196), calls=%async_computation.2 | async-start | bytes 3670016 | tf_op jit(solution)/shard_map/all_to_all | solution.py:72
  17.4 1.5 reshape.191
  18.9 39.3 %all-to-all-done.2 = bf16[32,6,3584]{2,1,0:T(8,128)(2,1)S(1)} async-done(((bf16[32,6,3584]{2,1,0:T(8,128)(2,1)}), bf16[32,6,3584]{2,1,0:T(8,128)(2,1)S(1)}, u32[]{:S(2)}, u32[]{:S(2)}) %all-to-all-start.2) | async-done | bytes 1376288 | tf_op jit(solution)/shard_map/all_to_all | solution.py:72
  58.1 4.7 %all-to-all-start = ((bf16[32,6,3584]{2,1,0:T(8,128)(2,1)}), bf16[32,6,3584]{2,1,0:T(8,128)(2,1)}, u32[]{:S(2)}, u32[]{:S(2)}) async-start(bf16[32,6,3584]{2,1,0:T(8,128)(2,1)} %reshape.191), calls=%async_computation | async-start | bytes 3670016 | tf_op jit(solution)/shard_map/all_to_all | solution.py:72
  63.3 8.2 %fusion.11 = bf16[192,3584]{1,0:T(8,128)(2,1)S(1)} fusion(bf16[1,1024,3584]{2,1,0:T(8,128)(2,1)} %param.23, bf16[192,3584]{1,0:T(8,128)(2,1)S(1)} %reshape.197, bf16[1,3584,1024]{2,1,0:T(8,128)(2,1)} %param.22), kind=kOutput, calls=%fused_computation.13 | convolution fusion | flops 2820243456 | bytes 17432576 | tf_op jit(solution)/shard_map/dot_general | solution.py:77
  71.6 1.5 reshape.198
  73.1 32.4 %all-to-all-done = bf16[32,6,3584]{2,1,0:T(8,128)(2,1)} async-done(((bf16[32,6,3584]{2,1,0:T(8,128)(2,1)}), bf16[32,6,3584]{2,1,0:T(8,128)(2,1)}, u32[]{:S(2)}, u32[]{:S(2)}) %all-to-all-start) | async-done | bytes 1376288 | tf_op jit(solution)/shard_map/all_to_all | solution.py:72
  105.5 4.6 %all-to-all-start.3 = ((bf16[32,6,3584]{2,1,0:T(8,128)(2,1)}), bf16[32,6,3584]{2,1,0:T(8,128)(2,1)S(1)}, u32[]{:S(2)}, u32[]{:S(2)}) async-start(bf16[32,6,3584]{2,1,0:T(8,128)(2,1)} %reshape.198), calls=%async_computation.3 | async-start | bytes 3670016 | tf_op jit(solution)/shard_map/all_to_all | solution.py:81
  110.1 2.5 %reshape.192 = bf16[192,3584]{1,0:T(8,128)(2,1)S(1)} reshape(bf16[32,6,3584]{2,1,0:T(8,128)(2,1)} %all-to-all-done) | data formatting | bytes 2752512 | tf_op jit(solution)/shard_map/reshape | solution.py:73
  112.6 9.3 %fusion.8 = bf16[192,3584]{1,0:T(8,128)(2,1)} fusion(bf16[1,1024,3584]{2,1,0:T(8,128)(2,1)} %param.23, bf16[192,3584]{1,0:T(8,128)(2,1)S(1)} %reshape.192, bf16[1,3584,1024]{2,1,0:T(8,128)(2,1)} %param.22), kind=kOutput, calls=%fused_computation.12 | convolution fusion | flops 2820243456 | bytes 17432576 | tf_op jit(solution)/shard_map/dot_general | solution.py:77
  121.9 3.4 %reshape.193 = bf16[32,6,3584]{2,1,0:T(8,128)(2,1)} reshape(bf16[192,3584]{1,0:T(8,128)(2,1)} %fusion.8) | data formatting | bytes 2752512 | tf_op jit(solution)/shard_map/reshape | solution.py:80
  125.4 27.4 %all-to-all-done.3 = bf16[32,6,3584]{2,1,0:T(8,128)(2,1)S(1)} async-done(((bf16[32,6,3584]{2,1,0:T(8,128)(2,1)}), bf16[32,6,3584]{2,1,0:T(8,128)(2,1)S(1)}, u32[]{:S(2)}, u32[]{:S(2)}) %all-to-all-start.3) | async-done | bytes 1376288 | tf_op jit(solution)/shard_map/all_to_all | solution.py:81
  152.7 4.7 %all-to-all-start.1 = ((bf16[32,6,3584]{2,1,0:T(8,128)(2,1)}), bf16[32,6,3584]{2,1,0:T(8,128)(2,1)}, u32[]{:S(2)}, u32[]{:S(2)}) async-start(bf16[32,6,3584]{2,1,0:T(8,128)(2,1)} %reshape.193), calls=%async_computation.1 | async-start | bytes 3670016 | tf_op jit(solution)/shard_map/all_to_all | solution.py:81
  158.2 7.2 %convolution_bitcast_fusion = f32[1,16,3584]{2,1,0:T(8,128)S(1)} fusion(bf16[1024,3584]{1,0:T(8,128)(2,1)} %param.25, bf16[3584,1024]{1,0:T(8,128)(2,1)} %param.24, bf16[2,16,3584]{2,1,0:T(8,128)(2,1)S(1)} %copy-done.2), kind=kOutput, calls=%fused_computation.16 | convolution fusion | flops 234962944 | bytes 15024128 | tf_op jit(solution)/shard_map/dot_general | solution.py:96
  165.4 7.9 %convolution_bitcast_fusion.1 = f32[1,16,3584]{2,1,0:T(8,128)} fusion(bf16[1024,3584]{1,0:T(8,128)(2,1)} %param.25, bf16[3584,1024]{1,0:T(8,128)(2,1)} %param.24, bf16[2,16,3584]{2,1,0:T(8,128)(2,1)S(1)} %copy-done.2), kind=kOutput, calls=%fused_computation.17 | convolution fusion | flops 234962944 | bytes 15024128 | tf_op jit(solution)/shard_map/dot_general | solution.py:96
  173.9 2.0 gather_fusion.3
  175.9 24.3 %all-to-all-done.1 = bf16[32,6,3584]{2,1,0:T(8,128)(2,1)} async-done(((bf16[32,6,3584]{2,1,0:T(8,128)(2,1)}), bf16[32,6,3584]{2,1,0:T(8,128)(2,1)}, u32[]{:S(2)}, u32[]{:S(2)}) %all-to-all-start.1) | async-done | bytes 1376288 | tf_op jit(solution)/shard_map/all_to_all | solution.py:81
  200.2 2.4 %reshape.194 = bf16[192,3584]{1,0:T(8,128)(2,1)S(1)} reshape(bf16[32,6,3584]{2,1,0:T(8,128)(2,1)} %all-to-all-done.1) | data formatting | bytes 2752512 | tf_op jit(solution)/shard_map/reshape | solution.py:84
  202.6 1.1 gather_fusion.1
  204.5 0.7 bitcast_reduce_fusion.1
  205.3 1.7 fusion.23
  (62 shorter events, 9.0 us)
Async XLA Ops:
  8.4 8.4 %copy-start.1 = (bf16[2,16,3584]{2,1,0:T(8,128)(2,1)S(1)}, bf16[2,16,3584]{2,1,0:T(8,128)(2,1)}, u32[]{:S(2)}) copy-start(bf16[2,16,3584]{2,1,0:T(8,128)(2,1)} %param.17) | copy-start | bytes 688132
  8.4 49.7 %all-to-all-start.2 = ((bf16[32,6,3584]{2,1,0:T(8,128)(2,1)}), bf16[32,6,3584]{2,1,0:T(8,128)(2,1)S(1)}, u32[]{:S(2)}, u32[]{:S(2)}) async-start(bf16[32,6,3584]{2,1,0:T(8,128)(2,1)} %reshape.196), calls=%async_computation.2 | async-start | bytes 3670016 | tf_op jit(solution)/shard_map/all_to_all | solution.py:72
  58.1 47.4 %all-to-all-start = ((bf16[32,6,3584]{2,1,0:T(8,128)(2,1)}), bf16[32,6,3584]{2,1,0:T(8,128)(2,1)}, u32[]{:S(2)}, u32[]{:S(2)}) async-start(bf16[32,6,3584]{2,1,0:T(8,128)(2,1)} %reshape.191), calls=%async_computation | async-start | bytes 3670016 | tf_op jit(solution)/shard_map/all_to_all | solution.py:72
  105.5 47.2 %all-to-all-start.3 = ((bf16[32,6,3584]{2,1,0:T(8,128)(2,1)}), bf16[32,6,3584]{2,1,0:T(8,128)(2,1)S(1)}, u32[]{:S(2)}, u32[]{:S(2)}) async-start(bf16[32,6,3584]{2,1,0:T(8,128)(2,1)} %reshape.198), calls=%async_computation.3 | async-start | bytes 3670016 | tf_op jit(solution)/shard_map/all_to_all | solution.py:81
  121.9 35.5 %copy-start.3 = (f32[2,16,8]{1,2,0:T(8,128)S(1)}, f32[2,16,8]{1,2,0:T(8,128)}, u32[]{:S(2)}) copy-start(f32[2,16,8]{1,2,0:T(8,128)} %param.21) | copy-start | bytes 3076
  121.9 36.3 %copy-start.2 = (bf16[2,16,3584]{2,1,0:T(8,128)(2,1)S(1)}, bf16[2,16,3584]{2,1,0:T(8,128)(2,1)}, u32[]{:S(2)}) copy-start(bf16[2,16,3584]{2,1,0:T(8,128)(2,1)} %param.17) | copy-start | bytes 688132
  152.7 47.5 %all-to-all-start.1 = ((bf16[32,6,3584]{2,1,0:T(8,128)(2,1)}), bf16[32,6,3584]{2,1,0:T(8,128)(2,1)}, u32[]{:S(2)}, u32[]{:S(2)}) async-start(bf16[32,6,3584]{2,1,0:T(8,128)(2,1)} %reshape.193), calls=%async_computation.1 | async-start | bytes 3670016 | tf_op jit(solution)/shard_map/all_to_all | solution.py:81
  202.6 1.2 copy-start
where the time goes:
time: 209 us; the launch traced here: 207 us
  waiting for transfers between devices  123 us (59%)
  matrix products  34.7 us (17%)
  local copies, waits for them, and re-layouts  22.3 us (11%)
  starting transfers between devices  21.1 us (10%)
  other arithmetic  5.25 us (3%)
    all_to_all x2, waiting for transfers between devices, shards(): lax.all_to_all(batch, 'expert', split_axis=0, concat_axis=0, tiled=True)  71.7 us
    all_to_all x2, waiting for transfers between devices, shards(): lax.all_to_all(partial_value, 'expert', split_axis=0, concat_axis=0, tile...  51.7 us
    dot_general x2, matrix products, shards(): jnp.dot(hidden, slot_down[0], preferred_element_type=jnp.float32)  17.5 us
    dot_general x2, matrix products, shards(): jnp.dot(shared_act, shared_down, preferred_element_type=jnp.float32)  15.1 us
    all_to_all x2, starting transfers between devices, shards(): lax.all_to_all(batch, 'expert', split_axis=0, concat_axis=0, tiled=True)  11.8 us
    all_to_all x2, starting transfers between devices, shards(): lax.all_to_all(partial_value, 'expert', split_axis=0, concat_axis=0, tile...  9.34 us
    reshape x2, local copies, waits for them, and re-layouts, shards(): partial_value = partial_value.reshape(received.shape[0], -1, width_full)  4.93 us
  transfers between devices with their start and end apart: 4, of which 4 were waited for; matrix products, arithmetic and copies ran while one was open for 23% of the time, Pallas kernels for 0%

commit v1 on v0

v1 whole, which is shorter than its diff:
```python
import jax
import jax.numpy as jnp
from jax import lax
from jax.sharding import PartitionSpec as P


def slot_gains(lengths, chosen, second, gains, slot_count):
    row_count = chosen.shape[1]
    span = row_count // lengths.shape[1]
    replicas = slot_count // 8
    experts_all = slot_count - replicas
    limit = jnp.repeat(lengths, span, axis=1, total_repeat_length=row_count)
    live = (jnp.arange(row_count, dtype=jnp.int32)[None] % span < limit).astype(jnp.float32)
    slot = jnp.where((chosen < replicas) & (second == 1), chosen + experts_all, chosen)
    hit = slot[..., None] == jnp.arange(slot_count, dtype=jnp.int32)
    dense = jnp.sum(jnp.where(hit, gains[..., None], 0.0), axis=2)
    return live, dense * live[..., None]


def shards(
    hidden_rows,
    draft_len,
    expert_ids,
    replica,
    route_gain,
    slot_up,
    slot_down,
    shared_up,
    shared_down,
):
    slot_count = lax.axis_size("expert")
    me = lax.axis_index("expert")
    steps, rows, _ = hidden_rows.shape
    own = lax.all_gather(hidden_rows, "tensor", axis=2, tiled=True)
    width = own.shape[2]
    live, dense = slot_gains(draft_len, expert_ids, replica, route_gain, slot_count)
    high = dense.astype(jnp.bfloat16)
    low = (dense - high.astype(jnp.float32)).astype(jnp.bfloat16)
    packed = jnp.concatenate([own, high, low], axis=2)
    routed = []
    for index in range(steps):
        everything = lax.all_gather(packed[index], "expert", axis=0, tiled=True)
        source = everything[:, :width]
        pick = jnp.arange(slot_count) == me
        both = everything[:, width:].astype(jnp.float32)
        both = both[:, :slot_count] + both[:, slot_count:]
        weight = jnp.sum(jnp.where(pick[None], both, 0.0), axis=1, keepdims=True)
        hidden = jax.nn.silu(
            jnp.dot(source, slot_up[0], preferred_element_type=jnp.float32)
        ).astype(jnp.bfloat16)
        part = jnp.dot(hidden, slot_down[0], preferred_element_type=jnp.float32)
        part = (part * weight).astype(jnp.bfloat16)
        part = lax.psum_scatter(part, "tensor", scatter_dimension=1, tiled=True)
        routed.append(lax.psum_scatter(part, "expert", scatter_dimension=0, tiled=True))
    flat = own.reshape(steps * rows, width)
    shared_act = jax.nn.silu(
        jnp.dot(flat, shared_up, preferred_element_type=jnp.float32)
    ).astype(jnp.bfloat16)
    shared_out = jnp.dot(shared_act, shared_down, preferred_element_type=jnp.float32)
    if lax.axis_size("tensor") > 1:
        shared_out = lax.psum_scatter(shared_out, "tensor", scatter_dimension=1, tiled=True)
    shared_out = shared_out.reshape(steps, rows, -1)
    total = jnp.stack(routed).astype(jnp.float32) + shared_out
    return (total * live[..., None]).astype(jnp.bfloat16)


def solution(mesh):
    return jax.shard_map(
        shards,
        mesh=mesh,
        in_specs=(
            P(None, "expert", "tensor"),
            P(None, "expert"),
            P(None, "expert", None),
            P(None, "expert", None),
            P(None, "expert", None),
            P("expert", None, "tensor"),
            P("expert", "tensor", None),
            P(None, "tensor"),
            P("tensor", None),
        ),
        out_specs=P(None, "expert", "tensor"),
        check_vma=False,
    )
```

time: 209 us -> 441 us (2.11)
  waiting for transfers between devices: 123 us -> 369 us
  starting transfers between devices: 21.1 us -> 0.12 us
  local copies, waits for them, and re-layouts: 22.3 us -> 4.91 us
  between operations: 0.27 us -> 13.2 us
  matrix products: 34.7 us -> 41.7 us
    reduce_scatter x0 -> x2, waiting for transfers between devices: none -> 244 us  [shards(): lax.psum_scatter(part, 'expert', scatter_dimension=0, tiled=True)]
    all_gather x0 -> x2, waiting for transfers between devices: none -> 124 us  [shards(): everything = lax.all_gather(packed[index], 'expert', axis=0, tiled=True)]
    all_to_all x4 -> x0, waiting for transfers between devices: 123 us -> none  [the longest x2 71.7 us: shards(): lax.all_to_all(batch, 'expert', split_axis=0, concat_axis=0, tiled=True)]
    all_to_all x4 -> x0, starting transfers between devices: 21.1 us -> none  [the longest x2 11.8 us: shards(): lax.all_to_all(batch, 'expert', split_axis=0, concat_axis=0, tiled=True)]
    dot_general x4, matrix products: 19.6 us -> 33.8 us  [the longest x2 17 us: shards(): part = jnp.dot(hidden, slot_down[0], preferred_element_type=jnp.float32)]
    reshape x8 -> x0, local copies, waits for them, and re-layouts: 13.8 us -> none  [the longest x2 4.93 us: shards(): partial_value = partial_value.reshape(received.shape[0], -1, width_full)]
    dot_general x2 -> x1, matrix products: 15.1 us -> 7.89 us  [shards(): jnp.dot(shared_act, shared_down, preferred_element_type=jnp.float32)]
  transfers between devices with their start and end apart: 4 -> 4, of which waited for: 4 -> 4; matrix products, arithmetic and copies ran while one was open for 23% -> 6% of each run, Pallas kernels for 0% -> 0%
where the time goes in v1:
time: 441 us; the launch traced here: 435 us
  waiting for transfers between devices  369 us (84%)
  matrix products  41.7 us (9%)
  between operations  13.2 us (3%)
  other arithmetic  5.64 us (1%)
  local copies, waits for them, and re-layouts  4.91 us (1%)
    reduce_scatter x2, waiting for transfers between devices, shards(): lax.psum_scatter(part, 'expert', scatter_dimension=0, tiled=True)  244 us
    all_gather x2, waiting for transfers between devices, shards(): everything = lax.all_gather(packed[index], 'expert', axis=0, tiled=True)  124 us
    dot_general x2, matrix products, shards(): part = jnp.dot(hidden, slot_down[0], preferred_element_type=jnp.float32)  17 us
    dot_general x2, matrix products, shards(): jnp.dot(source, slot_up[0], preferred_element_type=jnp.float32)  16.8 us
  transfers between devices with their start and end apart: 4, of which 4 were waited for; matrix products, arithmetic and copies ran while one was open for 6% of the time, Pallas kernels for 0%

profile of v1, /device:TPU:1, one launch (start us, length us, event | category | flops | bytes accessed | tf_op | source)
XLA Modules:
  0.0 435.0 jit_solution(3285700499009849925)
XLA Ops:
  6.5 0.7 pad_clamp_fusion
  7.2 0.8 copy.17
  8.0 0.6 gather_fusion
  8.6 0.1 copy.18
  8.7 0.7 add_select_fusion
  9.5 0.8 copy.16
  10.3 0.1 select_reduce_fusion
  10.5 1.0 concatenate.7
  11.5 0.7 fusion.29
  12.3 0.7 all-gather.5.cloned.1.call-update
  13.1 62.8 %all-gather.7.cloned.1.call-done = bf16[1,512,3648]{2,1,0:T(8,128)(2,1)} async-done(((bf16[1,16,3648]{2,1,0:T(8,128)(2,1)}), bf16[1,512,3648]{2,1,0:T(8,128)(2,1)}) %all-gather.7.cloned.1.call-update) | async-done | bytes 3735568 | tf_op jit(solution)/shard_map/all_gather | solution.py:42
  75.8 0.9 slice_convert_fusion
  76.7 61.6 %all-gather.5.cloned.1.call-done = bf16[1,512,3648]{2,1,0:T(8,128)(2,1)} async-done(((bf16[1,16,3648]{2,1,0:T(8,128)(2,1)}), bf16[1,512,3648]{2,1,0:T(8,128)(2,1)}) %all-gather.5.cloned.1.call-update) | async-done | bytes 3735568 | tf_op jit(solution)/shard_map/all_gather | solution.py:42
  138.3 0.9 slice_convert_fusion.1
  139.3 8.4 %multiply_convert_fusion.3 = bf16[512,1024]{1,0:T(8,128)(2,1)S(1)} fusion(bf16[1,3584,1024]{2,1,0:T(8,128)(2,1)} %param.16, bf16[512,3648]{1,0:T(8,128)(2,1)} %bitcast.38), kind=kOutput, calls=%fused_computation.14 | convolution fusion | flops 3760717824 | bytes 12058624 | tf_op jit(solution)/shard_map/dot_general | solution.py:49
  147.7 0.4 fusion.25
  148.1 8.5 %multiply_convert_fusion.1 = bf16[512,3584]{1,0:T(8,128)(2,1)} fusion(bf16[512,1024]{1,0:T(8,128)(2,1)S(1)} %multiply_convert_fusion.3, bf16[1,1024,3584]{2,1,0:T(8,128)(2,1)} %param.17, f32[512]{0:T(512)S(1)} %get-tuple-element.17), kind=kOutput, calls=%fused_computation.10 | convolution fusion | flops 3761766400 | bytes 12060672 | tf_op jit(solution)/shard_map/dot_general | solution.py:51
  156.7 8.4 %multiply_convert_fusion.2 = bf16[512,1024]{1,0:T(8,128)(2,1)S(1)} fusion(bf16[1,3584,1024]{2,1,0:T(8,128)(2,1)} %param.16, bf16[512,3648]{1,0:T(8,128)(2,1)} %bitcast.36), kind=kOutput, calls=%fused_computation.13 | convolution fusion | flops 3760717824 | bytes 12058624 | tf_op jit(solution)/shard_map/dot_general | solution.py:49
  165.1 8.5 %multiply_convert_fusion = bf16[512,3584]{1,0:T(8,128)(2,1)} fusion(bf16[512,1024]{1,0:T(8,128)(2,1)S(1)} %multiply_convert_fusion.2, bf16[1,1024,3584]{2,1,0:T(8,128)(2,1)} %param.17, f32[512]{0:T(512)S(1)} %get-tuple-element.18), kind=kOutput, calls=%fused_computation.9 | convolution fusion | flops 3761766400 | bytes 12060672 | tf_op jit(solution)/shard_map/dot_general | solution.py:51
  173.6 0.9 copy-done
  174.5 7.9 %fusion.26 = f32[32,3584]{1,0:T(8,128)S(1)} fusion(bf16[1024,3584]{1,0:T(8,128)(2,1)} %param.19, bf16[32,3584]{1,0:T(8,128)(2,1)S(1)} %bitcast.32, bf16[3584,1024]{1,0:T(8,128)(2,1)} %param.18), kind=kOutput, calls=%fused_computation.27 | convolution fusion | flops 469925888 | bytes 15368192 | tf_op jit(solution)/shard_map/dot_general | solution.py:59
  182.4 106.8 %reduce-scatter.3.cloned.1.call-done = bf16[16,3584]{1,0:T(8,128)(2,1)} async-done(((bf16[512,3584]{1,0:T(8,128)(2,1)}), bf16[16,3584]{1,0:T(8,128)(2,1)}) %reduce-scatter.3.cloned.1.call-update) | async-done | bytes 114704 | tf_op jit(solution)/shard_map/reduce_scatter | solution.py:54
  289.1 137.6 %reduce-scatter.5.cloned.1.call-done = bf16[16,3584]{1,0:T(8,128)(2,1)} async-done(((bf16[512,3584]{1,0:T(8,128)(2,1)}), bf16[16,3584]{1,0:T(8,128)(2,1)}) %reduce-scatter.5.cloned.1.call-update) | async-done | bytes 114704 | tf_op jit(solution)/shard_map/reduce_scatter | solution.py:54
  426.7 1.7 multiply_convert_fusion.4
  (13 shorter events, 0.4 us)
Async XLA Ops:
  6.5 69.3 %all-gather.7.cloned.1.call-start = ((), (), s32[]{:S(2)}) async-start(), calls=%async_computation.5 | async-start | bytes 3919872 | tf_op jit(solution)/shard_map/all_gather | solution.py:42
  12.2 126.1 %all-gather.5.cloned.1.call-start = ((), (), s32[]{:S(2)}) async-start(), calls=%async_computation.4 | async-start | bytes 3919872 | tf_op jit(solution)/shard_map/all_gather | solution.py:42
  13.0 276.1 %reduce-scatter.3.cloned.1.call-start = ((), (), s32[]{:S(2)}) async-start(), calls=%async_computation.2 | async-start | bytes 3784704 | tf_op jit(solution)/shard_map/reduce_scatter | solution.py:54
  156.6 270.1 %reduce-scatter.5.cloned.1.call-start = ((), (), s32[]{:S(2)}) async-start(), calls=%async_computation.3 | async-start | bytes 3784704 | tf_op jit(solution)/shard_map/reduce_scatter | solution.py:54
  173.5 0.9 copy-start
Sparse Core Ops, SparseCore 0:
  12.4 63.4 all-gather.6
  78.6 59.6 all-gather.4
  156.7 132.3 reduce-scatter.2
  291.4 135.2 reduce-scatter.4

commit v2 on v1

--- a/solution.py
+++ b/solution.py
@@ -1,7 +1,492 @@
+import functools
 import jax
 import jax.numpy as jnp
 from jax import lax
+from jax.experimental import pallas as pl
+from jax.experimental.pallas import tpu as pltpu
 from jax.sharding import PartitionSpec as P
+
+BF = jnp.bfloat16
+F32 = jnp.float32
+EXTRA = 128
+
+
+def mm(a, b):
+    return jnp.dot(a, b, preferred_element_type=F32)
+
+
+def silu(v):
+    return v / (1.0 + jnp.exp(-v))
+
+
+def fused(
+    x_ref, live_ref, up_hbm, down_hbm, sup_hbm, sdown_hbm, out_ref,
+    gat, part, swapped, from_f, from_s, from_up, from_dn, from_fin,
+    up, down, sup, sdown, hid, gain, shid, shout,
+    w_sem, swap_s, swap_r, zu_s, zd_s, d1_s, d2_s, ag_r, sib_s, sib_r,
+    x0_s, x0_r, f_s, f_r, s_s, s_r, ru_s, ru_r, rd_s, rd_r, fin_s, fin_r,
+):
+    steps = gat.shape[1]
+    chips = gat.shape[2]
+    rows = gat.shape[4]
+    half = part.shape[5]
+    lines = chips // 4
+    hidden_units = up.shape[1]
+    me = lax.axis_index("expert")
+    c = me % 2
+    chip = me // 2
+    x = chip % 2
+    y = (chip // 2) % 2
+    z = chip // 4
+    d1 = x + c * (y - x)
+    d2 = y + c * (x - y)
+    w1 = 1 + c
+    w2 = 2 - c
+    turn = 1 - 2 * (z // (lines // 2))
+
+    def chip_of(zz, a, b):
+        return zz * 4 + a * w1 + b * w2
+
+    def order(k):
+        return (z + turn * k + lines) % lines
+
+    sib = chip * 2 + (1 - c)
+    above = me + 8
+    below = me - 8
+    n1 = chip_of(z, 1 - d1, d2) * 2 + c
+    n2 = chip_of(z, d1, 1 - d2) * 2 + c
+
+    def send(src, dst, ssem, rsem, dev):
+        return pltpu.make_async_remote_copy(
+            src_ref=src, dst_ref=dst, send_sem=ssem, recv_sem=rsem,
+            device_id=(dev, 0), device_id_type=pl.DeviceIdType.MESH,
+        )
+
+    barrier = pltpu.get_barrier_semaphore()
+
+    def greet(dev):
+        pl.semaphore_signal(
+            barrier, inc=1, device_id=(dev, 0), device_id_type=pl.DeviceIdType.MESH
+        )
+
+    loads = [
+        pltpu.make_async_copy(src, dst, w_sem.at[i])
+        for i, (src, dst) in enumerate(
+            [(sup_hbm, sup), (sdown_hbm, sdown), (up_hbm.at[0], up), (down_hbm.at[0], down)]
+        )
+    ]
+    loads[0].start()
+    loads[1].start()
+    loads[2].start()
+    loads[3].start()
+    for dev in (sib, n1, n2):
+        greet(dev)
+
+    @pl.when(z > 0)
+    def _():
+        greet(below)
+
+    @pl.when(z < lines - 1)
+    def _():
+        greet(above)
+
+    pl.semaphore_wait(barrier, 3 + jnp.minimum(z, 1) + jnp.minimum(lines - 1 - z, 1))
+
+    def swap(s):
+        return send(
+            x_ref.at[1 - c, s], gat.at[1 - c, s, chip, c], swap_s.at[s], swap_r.at[s], sib
+        )
+
+    def block(s, who):
+        return gat.at[c, s, who]
+
+    def go_up(s, zz):
+        b = block(s, chip_of(zz, d1, d2))
+        return send(b, b, zu_s.at[s, zz], ag_r.at[s, chip_of(zz, d1, d2)], above)
+
+    def go_dn(s, zz):
+        b = block(s, chip_of(zz, d1, d2))
+        return send(b, b, zd_s.at[s, zz], ag_r.at[s, chip_of(zz, d1, d2)], below)
+
+    def go_d1(s, zz):
+        b = block(s, chip_of(zz, d1, d2))
+        return send(b, b, d1_s.at[s, zz], ag_r.at[s, chip_of(zz, d1, d2)], n1)
+
+    def go_d2(s, a, zz):
+        b = block(s, chip_of(zz, a, d2))
+        return send(b, b, d2_s.at[s, a * lines + zz], ag_r.at[s, chip_of(zz, a, d2)], n2)
+
+    def go_sib(s, who):
+        b = block(s, who)
+        return send(b, b, sib_s.at[s, who], sib_r.at[s, who], sib)
+
+    def arrived(s, who):
+        b = block(s, who)
+        send(b, b, sib_s.at[s, who], ag_r.at[s, who], sib).wait_recv()
+
+    def spread(s, zz):
+        go_d1(s, zz).start()
+        go_d2(s, d1, zz).start()
+        go_sib(s, chip_of(zz, d1, d2)).start()
+
+    def ag_own(s):
+        swap(s).wait_recv()
+
+        @pl.when(z < lines - 1)
+        def _():
+            go_up(s, z).start()
+
+        @pl.when(z > 0)
+        def _():
+            go_dn(s, z).start()
+
+        spread(s, z)
+
+    def ag_line(s):
+        for d in range(1, lines):
+            @pl.when(z - d >= 0)
+            def _():
+                arrived(s, chip_of(z - d, d1, d2))
+
+                @pl.when(z < lines - 1)
+                def _():
+                    go_up(s, z - d).start()
+
+                spread(s, z - d)
+
+            @pl.when(z + d < lines)
+            def _():
+                arrived(s, chip_of(z + d, d1, d2))
+
+                @pl.when(z > 0)
+                def _():
+                    go_dn(s, z + d).start()
+
+                spread(s, z + d)
+
+    def ag_d1(s, k):
+        zz = order(k)
+        arrived(s, chip_of(zz, 1 - d1, d2))
+        go_d2(s, 1 - d1, zz).start()
+        go_sib(s, chip_of(zz, 1 - d1, d2)).start()
+
+    def ag_d2(s, m):
+        a = (d1 + m // lines) % 2
+        who = chip_of(order(m % lines), a, 1 - d2)
+        arrived(s, who)
+        go_sib(s, who).start()
+
+    def loop(n, body):
+        def step(i, carry):
+            body(i)
+            return carry
+
+        lax.fori_loop(0, n, step, 0)
+
+    def ag_finish(s):
+        def one(who):
+            b = gat.at[1 - c, s, who]
+            send(b, b, sib_s.at[s, who], sib_r.at[s, who], sib).wait_recv()
+
+        loop(chips, one)
+
+    def cut(i, n):
+        return pl.ds(pl.multiple_of(i * n, n), n)
+
+    def shared_up_chunk(i):
+        cols = cut(i, 256)
+        v = mm(x_ref[0, :, :, :half].reshape(steps * rows, half), sup[:half, cols])
+        v = v + mm(x_ref[1, :, :, :half].reshape(steps * rows, half), sup[half:, cols])
+        shid[:, cols] = silu(v).astype(BF)
+
+    def shared_down_chunk(j):
+        cols = cut(j, 512)
+        shout[:, cols] = mm(shid[...], sdown[:, cols])
+
+    def gains(s):
+        lane = lax.broadcasted_iota(jnp.int32, (chips * 2 * rows, EXTRA), 1)
+        both = gat[0, s, :, :, :, half:].astype(F32) + gat[1, s, :, :, :, half:].astype(F32)
+        both = both.reshape(chips * 2 * rows, EXTRA)
+        gain[...] = jnp.sum(jnp.where(lane == me, both, 0.0), axis=1, keepdims=True)
+
+    def up_chunk(s, i):
+        cols = cut(i, 256)
+        v = mm(gat[0, s, :, :, :, :half].reshape(chips * 2 * rows, half), up[:half, cols])
+        v = v + mm(gat[1, s, :, :, :, :half].reshape(chips * 2 * rows, half), up[half:, cols])
+        hid[:, cols] = silu(v).astype(BF)
+
+    def down_chunk(s, h, j):
+        v = mm(hid[...], down[:, pl.ds(pl.multiple_of(h * half + j * 256, 256), 256)])
+        v = (v * gain[...]).astype(BF)
+        part[h, s, :, :, :, cut(j, 256)] = v.reshape(chips, 2, rows, 256)
+
+    def x0(s):
+        return send(part.at[1 - c, s], swapped.at[s], x0_s.at[s], x0_r.at[s], sib)
+
+    def both_cores(s, who):
+        return part[c, s, who].astype(F32) + swapped[s, who].astype(F32)
+
+    def f_copy(s, a, zz):
+        who = chip_of(zz, a, 1 - d2)
+        i = a * lines + zz
+        return send(part.at[c, s, who], from_f.at[s, i], f_s.at[s, i], f_r.at[s, i], n2)
+
+    def rs_f(s, q):
+        a = (1 - d1 + q // lines) % 2
+        zz = order(q % lines)
+        who = chip_of(zz, a, 1 - d2)
+        part[c, s, who] = both_cores(s, who).astype(BF)
+        f_copy(s, a, zz).start()
+
+    def with_f(s, a, zz):
+        f_copy(s, a, zz).wait_recv()
+        who = chip_of(zz, a, d2)
+        return both_cores(s, who) + from_f[s, a * lines + zz].astype(F32)
+
+    def s_copy(s, zz):
+        who = chip_of(zz, 1 - d1, d2)
+        return send(part.at[c, s, who], from_s.at[s, zz], s_s.at[s, zz], s_r.at[s, zz], n1)
+
+    def rs_s(s, k):
+        zz = order(k)
+        who = chip_of(zz, 1 - d1, d2)
+        part[c, s, who] = with_f(s, 1 - d1, zz).astype(BF)
+        s_copy(s, zz).start()
+
+    def up_copy(s, zz):
+        who = chip_of(zz, d1, d2)
+        return send(part.at[c, s, who], from_up.at[s, zz], ru_s.at[s, zz], ru_r.at[s, zz], above)
+
+    def dn_copy(s, zz):
+        who = chip_of(zz, d1, d2)
+        return send(part.at[c, s, who], from_dn.at[s, zz], rd_s.at[s, zz], rd_r.at[s, zz], below)
+
+    def rs_z(s):
+        def collect(k):
+            zz = order(k)
+            who = chip_of(zz, d1, d2)
+            v = with_f(s, d1, zz)
+            s_copy(s, zz).wait_recv()
+            part[c, s, who] = (v + from_s[s, zz].astype(F32)).astype(BF)
+
+        loop(lines, collect)
+        for d in range(lines - 1, 0, -1):
+            @pl.when(z + d < lines)
+            def _():
+                zz = z + d
+                who = chip_of(zz, d1, d2)
+
+                @pl.when(z > 0)
+                def _():
+                    up_copy(s, zz).wait_recv()
+                    v = part[c, s, who].astype(F32) + from_up[s, zz].astype(F32)
+                    part[c, s, who] = v.astype(BF)
+
+                up_copy(s, zz).start()
+
+            @pl.when(z - d >= 0)
+            def _():
+                zz = z - d
+                who = chip_of(zz, d1, d2)
+
+                @pl.when(z < lines - 1)
+                def _():
+                    dn_copy(s, zz).wait_recv()
+                    v = part[c, s, who].astype(F32) + from_dn[s, zz].astype(F32)
+                    part[c, s, who] = v.astype(BF)
+
+                dn_copy(s, zz).start()
+
+    def fin(s):
+        return send(part.at[c, s, chip, 1 - c], from_fin.at[s], fin_s.at[s], fin_r.at[s], sib)
+
+    def rs_own(s):
+        @pl.when(z > 0)
+        def _():
+            up_copy(s, z).wait_recv()
+            v = part[c, s, chip].astype(F32) + from_up[s, z].astype(F32)
+            part[c, s, chip] = v.astype(BF)
+
+        @pl.when(z < lines - 1)
+        def _():
+            dn_copy(s, z).wait_recv()
+            v = part[c, s, chip].astype(F32) + from_dn[s, z].astype(F32)
+            part[c, s, chip] = v.astype(BF)
+
+        fin(s).start()
+
+    def write(s):
+        fin(s).wait_recv()
+        keep = part[c, s, chip, c].astype(F32)
+        other = from_fin[s].astype(F32)
+        lead = jnp.where(c == 0, keep, other)
+        tail = jnp.where(c == 0, other, keep)
+        alive = live_ref[s, :, :1]
+        mine = pl.ds(s * rows, rows)
+        out_ref[s, :, :half] = ((lead + shout[mine, :half]) * alive).astype(out_ref.dtype)
+        out_ref[s, :, half:] = ((tail + shout[mine, half:]) * alive).astype(out_ref.dtype)
+
+    for s in range(steps):
+        gat[c, s, chip, c] = x_ref[c, s]
+        swap(s).start()
+    ag_own(0)
+    ag_line(0)
+    loads[0].wait()
+
+    def first(k):
+        ag_d1(0, k)
+        shared_up_chunk(k)
+
+    loop(lines, first)
+    ag_own(1)
+    ag_line(1)
+    loads[1].wait()
+
+    def second(m):
+        ag_d2(0, m)
+        shared_down_chunk(m)
+
+    loop(2 * lines - 1, second)
+    ag_d2(0, 2 * lines - 1)
+    ag_finish(0)
+    loads[2].wait()
+    gains(0)
+
+    def third(i):
+        up_chunk(0, i)
+        ag_d1(1, i)
+
+    loop(hidden_units // 256, third)
+    loads[3].wait()
+
+    def fourth(j):
+        down_chunk(0, 1 - c, j)
+        ag_d2(1, j)
+
+    loop(half // 256, fourth)
+    ag_d2(1, 2 * lines - 1)
+    x0(0).start()
+    loop(half // 256, lambda j: down_chunk(0, c, j))
+    x0(0).wait_recv()
+    loop(2 * lines, lambda q: rs_f(0, q))
+    ag_finish(1)
+    gains(1)
+    loop(hidden_units // 256, lambda i: up_chunk(1, i))
+
+    def fifth(j):
+        down_chunk(1, 1 - c, j)
+
+        @pl.when(j >= half // 256 - lines)
+        def _():
+            rs_s(0, j - (half // 256 - lines))
+
+    loop(half // 256, fifth)
+    x0(1).start()
+    loop(half // 256, lambda j: down_chunk(1, c, j))
+    x0(1).wait_recv()
+    loop(2 * lines, lambda q: rs_f(1, q))
+    rs_z(0)
+    loop(lines, lambda k: rs_s(1, k))
+    rs_own(0)
+    rs_z(1)
+    write(0)
+    rs_own(1)
+    write(1)
+
+    for s in range(steps):
+        swap(s).wait_send()
+        x0(s).wait_send()
+        fin(s).wait_send()
+
+        def planes(zz):
+            go_d1(s, zz).wait_send()
+            go_d2(s, 0, zz).wait_send()
+            go_d2(s, 1, zz).wait_send()
+            f_copy(s, 0, zz).wait_send()
+            f_copy(s, 1, zz).wait_send()
+            s_copy(s, zz).wait_send()
+
+            @pl.when((zz <= z) & (z < lines - 1))
+            def _():
+                go_up(s, zz).wait_send()
+
+            @pl.when((zz >= z) & (z > 0))
+            def _():
+                go_dn(s, zz).wait_send()
+
+            @pl.when(zz > z)
+            def _():
+                up_copy(s, zz).wait_send()
+
+            @pl.when(zz < z)
+            def _():
+                dn_copy(s, zz).wait_send()
+
+        loop(lines, planes)
+        loop(chips, lambda who: go_sib(s, who).wait_send())
+
+
+def fused_layer(
+    hidden_rows, draft_len, expert_ids, replica, route_gain, slot_up, slot_down, shared_up, shared_down
+):
+    slot_count = lax.axis_size("expert")
+    steps, rows, width = hidden_rows.shape
+    half = width // 2
+    chips = slot_count // 2
+    lines = chips // 4
+    hidden_units = slot_up.shape[2]
+    live, dense = slot_gains(draft_len, expert_ids, replica, route_gain, slot_count)
+    high = dense.astype(BF)
+    low = (dense - high.astype(F32)).astype(BF)
+    tail = jnp.pad(jnp.stack([high, low]), ((0, 0), (0, 0), (0, 0), (0, EXTRA - slot_count)))
+    halves = jnp.stack([hidden_rows[..., :half], hidden_rows[..., half:]])
+    packed = jnp.concatenate([halves, tail], axis=3)
+    alive = jnp.broadcast_to(live[..., None], (steps, rows, 128))
+    vm = pl.BlockSpec(memory_space=pltpu.VMEM)
+    hbm = pl.BlockSpec(memory_space=pl.ANY)
+    dma = pltpu.SemaphoreType.DMA
+    flops = 4 * steps * rows * (slot_count + 1) * width * hidden_units
+    return pl.pallas_call(
+        fused,
+        out_shape=jax.ShapeDtypeStruct((steps, rows, width), BF),
+        in_specs=[vm, vm, hbm, hbm, hbm, hbm],
+        out_specs=vm,
+        scratch_shapes=[
+            pltpu.VMEM((2, steps, chips, 2, rows, half + EXTRA), BF),
+            pltpu.VMEM((2, steps, chips, 2, rows, half), BF),
+            pltpu.VMEM((steps, chips, 2, rows, half), BF),
+            pltpu.VMEM((steps, 2 * lines, 2, rows, half), BF),
+            pltpu.VMEM((steps, lines, 2, rows, half), BF),
+            pltpu.VMEM((steps, lines, 2, rows, half), BF),
+            pltpu.VMEM((steps, lines, 2, rows, half), BF),
+            pltpu.VMEM((steps, rows, half), BF),
+            pltpu.VMEM(slot_up.shape[1:], BF),
+            pltpu.VMEM(slot_down.shape[1:], BF),
+            pltpu.VMEM(shared_up.shape, BF),
+            pltpu.VMEM(shared_down.shape, BF),
+            pltpu.VMEM((slot_count * rows, hidden_units), BF),
+            pltpu.VMEM((slot_count * rows, 1), F32),
+            pltpu.VMEM((steps * rows, shared_up.shape[1]), BF),
+            pltpu.VMEM((steps * rows, width), F32),
+            dma((4,)), dma((steps,)), dma((steps,)),
+            dma((steps, lines)), dma((steps, lines)), dma((steps, lines)),
+            dma((steps, 2 * lines)), dma((steps, chips)),
+            dma((steps, chips)), dma((steps, chips)),
+            dma((steps,)), dma((steps,)),
+            dma((steps, 2 * lines)), dma((steps, 2 * lines)),
+            dma((steps, lines)), dma((steps, lines)),
+            dma((steps, lines)), dma((steps, lines)),
+            dma((steps, lines)), dma((steps, lines)),
+            dma((steps,)), dma((steps,)),
+        ],
+        compiler_params=pltpu.CompilerParams(
+            collective_id=0, has_side_effects=True, vmem_limit_bytes=62 * 1024 * 1024
+        ),
+        cost_estimate=pl.CostEstimate(
+            flops=flops, bytes_accessed=4 * 2 * width * hidden_units, transcendentals=0
+        ),
+        name="fused_layer",
+    )(packed, alive, slot_up, slot_down, shared_up, shared_down)
 
 
 def slot_gains(lengths, chosen, second, gains, slot_count):
@@ -65,8 +550,9 @@
 
 
 def solution(mesh):
+    fits = mesh.shape["tensor"] == 1 and mesh.shape["expert"] == 32
     return jax.shard_map(
-        shards,
+        fused_layer if fits else shards,
         mesh=mesh,
         in_specs=(
             P(None, "expert", "tensor"),

time: 441 us -> 110 us (0.25); the launches traced: 435 us -> 110 us
  waiting for transfers between devices: 369 us -> 0 us
  Pallas kernels: 0 us -> 102 us
  matrix products: 41.7 us -> 0 us
  between operations: 13.2 us -> 0.04 us
    reduce_scatter x2 -> x0, waiting for transfers between devices: 244 us -> none  [shards(): lax.psum_scatter(part, 'expert', scatter_dimension=0, tiled=True)]
    all_gather x2 -> x0, waiting for transfers between devices: 124 us -> none  [shards(): everything = lax.all_gather(packed[index], 'expert', axis=0, tiled=True)]
    pallas_call x0 -> x1, Pallas kernels: none -> 102 us  [fused_layer(): pl.pallas_call(fused, out_shape=jax.ShapeDtypeStruct((steps, rows, width)...]
    dot_general x5 -> x0, matrix products: 41.7 us -> none  [the longest x2 17 us: shards(): part = jnp.dot(hidden, slot_down[0], preferred_element_type=jnp.float32)]
  transfers between devices with their start and end apart: 4 -> 0, of which waited for: 4 -> 0; matrix products, arithmetic and copies ran while one was open for 6% -> 0% of each run, Pallas kernels for 0% -> 0%
where the time goes in v2:
time: 110 us
  Pallas kernels  102 us (93%)
  local copies, waits for them, and re-layouts  5.54 us (5%)
  other arithmetic  2.39 us (2%)
    pallas_call x1, Pallas kernels, fused_layer(): pl.pallas_call(fused, out_shape=jax.ShapeDtypeStruct((steps, rows, width)...  102 us
    unnamed x3, local copies, waits for them, and re-layouts  3.18 us

profile of v2, /device:TPU:1, one launch (start us, length us, event | category | flops | bytes accessed | tf_op | source)
XLA Modules:
  0.0 109.9 jit_solution(15560720490046187184)
XLA Ops:
  0.0 0.7 pad_clamp_fusion
  0.7 0.8 copy.17
  1.4 0.6 gather_fusion
  2.0 0.1 convert_bitcast_fusion
  2.1 0.1 copy.18
  2.2 0.7 add_select_fusion
  2.9 0.1 copy.15
  2.9 0.8 copy.16
  3.7 0.1 select_reduce_fusion
  3.9 0.1 fusion.3
  4.0 1.0 slice_bitcast_fusion.1
  4.9 0.7 pad_maximum_fusion.x_ref
  5.6 0.7 broadcast_in_dim.22.live_ref
  6.3 101.9 %fused_layer.1 = bf16[2,16,3584]{2,1,0:T(8,128)(2,1)} custom-call(bf16[2,2,16,1920]{3,2,1,0:T(8,128)(2,1)} %pad_maximum_fusion.x_ref, f32[2,16,128]{2,1,0:T(8,128)} %broadcast_in_dim.22.live_ref, bf16[1,3584,1024]{2,1,0:T(8,128)(2,1)} %up_hbm.1, bf16[1,1024,3584]{2,1,0:T(8,128)(2,1)} %down_hbm.1, bf16[3584,1024]{1,0:T(8,128)(2,1)} %sup_hbm.1, ...), custom_call_target="tpu_custom_call" | custom-call | flops 15502147584 | bytes 29360128 | tf_op jit(solution)/shard_map/fused_layer/pallas_call | solution.py:449
  108.3 1.6 %copy.21 = bf16[2,16,3584]{2,1,0:T(8,128)(2,1)} copy(bf16[2,16,3584]{2,1,0:T(8,128)(2,1)} %fused_layer.1) | data formatting | bytes 458752
  (2 shorter events, 0.0 us)

commit v3 on v2

--- a/solution.py
+++ b/solution.py
@@ -20,8 +20,8 @@
 
 
 def fused(
-    x_ref, live_ref, up_hbm, down_hbm, sup_hbm, sdown_hbm, out_ref,
-    gat, part, swapped, from_f, from_s, from_up, from_dn, from_fin,
+    own_ref, len_ref, ids_ref, second_ref, gain_ref, up_hbm, down_hbm, sup_hbm, sdown_hbm,
+    out_ref, x_ref, live_ref, gat, part, swapped, from_f, from_s, from_up, from_dn, from_fin,
     up, down, sup, sdown, hid, gain, shid, shout,
     w_sem, swap_s, swap_r, zu_s, zd_s, d1_s, d2_s, ag_r, sib_s, sib_r,
     x0_s, x0_r, f_s, f_r, s_s, s_r, ru_s, ru_r, rd_s, rd_r, fin_s, fin_r,
@@ -90,6 +90,32 @@
     def _():
         greet(above)
 
+    slot_count = chips * 2
+    replicas = slot_count // 8
+    spans = len_ref.shape[1]
+    span = rows // spans
+    row_at = lax.broadcasted_iota(jnp.int32, (rows, spans), 0)
+    start_at = lax.broadcasted_iota(jnp.int32, (rows, spans), 1) * span
+    lane_at = lax.broadcasted_iota(jnp.int32, (rows, EXTRA), 1)
+    for s in range(steps):
+        lens = jnp.minimum(len_ref[pl.ds(s, 1), :], span)
+        inside = (row_at >= start_at) & (row_at < start_at + lens)
+        alive = jnp.sum(jnp.where(inside, 1.0, 0.0), axis=1, keepdims=True)
+        ids = ids_ref[s]
+        moved = (ids < replicas) & (second_ref[s] == 1)
+        slot = jnp.where(moved, ids + (slot_count - replicas), ids)
+        weights = gain_ref[s]
+        dense = jnp.zeros((rows, EXTRA), F32)
+        for k in range(ids.shape[1]):
+            dense = dense + jnp.where(lane_at == slot[:, k : k + 1], weights[:, k : k + 1], 0.0)
+        dense = dense * alive
+        high = dense.astype(BF)
+        x_ref[0, s, :, :half] = own_ref[s, :, :half]
+        x_ref[1, s, :, :half] = own_ref[s, :, half:]
+        x_ref[0, s, :, half:] = high
+        x_ref[1, s, :, half:] = (dense - high.astype(F32)).astype(BF)
+        live_ref[s] = jnp.broadcast_to(alive, (rows, 128))
+
     pl.semaphore_wait(barrier, 3 + jnp.minimum(z, 1) + jnp.minimum(lines - 1 - z, 1))
 
     def swap(s):
@@ -207,23 +233,42 @@
         lane = lax.broadcasted_iota(jnp.int32, (chips * 2 * rows, EXTRA), 1)
         both = gat[0, s, :, :, :, half:].astype(F32) + gat[1, s, :, :, :, half:].astype(F32)
         both = both.reshape(chips * 2 * rows, EXTRA)
-        gain[...] = jnp.sum(jnp.where(lane == me, both, 0.0), axis=1, keepdims=True)
+        mine = jnp.sum(jnp.where(lane == me, both, 0.0), axis=1, keepdims=True)
+        gain[...] = mine.reshape(chips, 2 * rows, 1)
 
     def up_chunk(s, i):
         cols = cut(i, 256)
         v = mm(gat[0, s, :, :, :, :half].reshape(chips * 2 * rows, half), up[:half, cols])
         v = v + mm(gat[1, s, :, :, :, :half].reshape(chips * 2 * rows, half), up[half:, cols])
-        hid[:, cols] = silu(v).astype(BF)
-
-    def down_chunk(s, h, j):
-        v = mm(hid[...], down[:, pl.ds(pl.multiple_of(h * half + j * 256, 256), 256)])
-        v = (v * gain[...]).astype(BF)
-        part[h, s, :, :, :, cut(j, 256)] = v.reshape(chips, 2, rows, 256)
-
-    def x0(s):
-        return send(part.at[1 - c, s], swapped.at[s], x0_s.at[s], x0_r.at[s], sib)
+        hid[:, :, cols] = silu(v).astype(BF).reshape(chips, 2 * rows, 256)
+
+    def members(t, far):
+        there = y + t * (x - y)
+        b = (1 - there) if far else there
+        return [
+            zz * 4 + a * (1 + t) + b * (2 - t) for zz in range(lines) for a in range(2)
+        ]
+
+    def down_chunk(s, t, far, j):
+        group = members(t, far)
+        source = jnp.concatenate([hid[who] for who in group], axis=0)
+        scale = jnp.concatenate([gain[who] for who in group], axis=0)
+        v = mm(source, down[:, pl.ds(pl.multiple_of(t * half + j * 256, 256), 256)])
+        v = (v * scale).astype(BF).reshape(len(group), 2, rows, 256)
+        for i, who in enumerate(group):
+            part[t, s, who, :, :, cut(j, 256)] = v[i]
+
+    def x0(s, who):
+        return send(
+            part.at[1 - c, s, who], swapped.at[s, who], x0_s.at[s, who], x0_r.at[s, who], sib
+        )
+
+    def x0_start(s, far):
+        for who in members(1 - c, far):
+            x0(s, who).start()
 
     def both_cores(s, who):
+        x0(s, who).wait_recv()
         return part[c, s, who].astype(F32) + swapped[s, who].astype(F32)
 
     def f_copy(s, a, zz):
@@ -358,33 +403,49 @@
 
     loop(hidden_units // 256, third)
     loads[3].wait()
+    chunks = half // 256
+    late = chunks - lines
+    loop(chunks, lambda j: down_chunk(0, 1 - c, True, j))
+    x0_start(0, True)
+    loop(chunks, lambda j: down_chunk(0, c, True, j))
+    loop(2 * lines, lambda q: rs_f(0, q))
 
     def fourth(j):
-        down_chunk(0, 1 - c, j)
-        ag_d2(1, j)
-
-    loop(half // 256, fourth)
-    ag_d2(1, 2 * lines - 1)
-    x0(0).start()
-    loop(half // 256, lambda j: down_chunk(0, c, j))
-    x0(0).wait_recv()
-    loop(2 * lines, lambda q: rs_f(0, q))
+        down_chunk(0, 1 - c, False, j)
+
+        @pl.when(j >= late)
+        def _():
+            ag_d2(1, j - late)
+
+    loop(chunks, fourth)
+    x0_start(0, False)
+
+    def fifth(j):
+        down_chunk(0, c, False, j)
+
+        @pl.when(j >= late)
+        def _():
+            ag_d2(1, j - late + lines)
+
+    loop(chunks, fifth)
     ag_finish(1)
     gains(1)
     loop(hidden_units // 256, lambda i: up_chunk(1, i))
 
-    def fifth(j):
-        down_chunk(1, 1 - c, j)
-
-        @pl.when(j >= half // 256 - lines)
+    def sixth(j):
+        down_chunk(1, 1 - c, True, j)
+
+        @pl.when(j >= late)
         def _():
-            rs_s(0, j - (half // 256 - lines))
-
-    loop(half // 256, fifth)
-    x0(1).start()
-    loop(half // 256, lambda j: down_chunk(1, c, j))
-    x0(1).wait_recv()
+            rs_s(0, j - late)
+
+    loop(chunks, sixth)
+    x0_start(1, True)
+    loop(chunks, lambda j: down_chunk(1, c, True, j))
     loop(2 * lines, lambda q: rs_f(1, q))
+    loop(chunks, lambda j: down_chunk(1, 1 - c, False, j))
+    x0_start(1, False)
+    loop(chunks, lambda j: down_chunk(1, c, False, j))
     rs_z(0)
     loop(lines, lambda k: rs_s(1, k))
     rs_own(0)
@@ -395,7 +456,6 @@
 
     for s in range(steps):
         swap(s).wait_send()
-        x0(s).wait_send()
         fin(s).wait_send()
 
         def planes(zz):
@@ -423,7 +483,12 @@
                 dn_copy(s, zz).wait_send()
 
         loop(lines, planes)
-        loop(chips, lambda who: go_sib(s, who).wait_send())
+
+        def siblings(who):
+            go_sib(s, who).wait_send()
+            x0(s, who).wait_send()
+
+        loop(chips, siblings)
 
 
 def fused_layer(
@@ -435,13 +500,6 @@
     chips = slot_count // 2
     lines = chips // 4
     hidden_units = slot_up.shape[2]
-    live, dense = slot_gains(draft_len, expert_ids, replica, route_gain, slot_count)
-    high = dense.astype(BF)
-    low = (dense - high.astype(F32)).astype(BF)
-    tail = jnp.pad(jnp.stack([high, low]), ((0, 0), (0, 0), (0, 0), (0, EXTRA - slot_count)))
-    halves = jnp.stack([hidden_rows[..., :half], hidden_rows[..., half:]])
-    packed = jnp.concatenate([halves, tail], axis=3)
-    alive = jnp.broadcast_to(live[..., None], (steps, rows, 128))
     vm = pl.BlockSpec(memory_space=pltpu.VMEM)
     hbm = pl.BlockSpec(memory_space=pl.ANY)
     dma = pltpu.SemaphoreType.DMA
@@ -449,9 +507,11 @@
     return pl.pallas_call(
         fused,
         out_shape=jax.ShapeDtypeStruct((steps, rows, width), BF),
-        in_specs=[vm, vm, hbm, hbm, hbm, hbm],
+        in_specs=[vm] * 5 + [hbm] * 4,
         out_specs=vm,
         scratch_shapes=[
+            pltpu.VMEM((2, steps, rows, half + EXTRA), BF),
+            pltpu.VMEM((steps, rows, 128), F32),
             pltpu.VMEM((2, steps, chips, 2, rows, half + EXTRA), BF),
             pltpu.VMEM((2, steps, chips, 2, rows, half), BF),
             pltpu.VMEM((steps, chips, 2, rows, half), BF),
@@ -464,15 +524,15 @@
             pltpu.VMEM(slot_down.shape[1:], BF),
             pltpu.VMEM(shared_up.shape, BF),
             pltpu.VMEM(shared_down.shape, BF),
-            pltpu.VMEM((slot_count * rows, hidden_units), BF),
-            pltpu.VMEM((slot_count * rows, 1), F32),
+            pltpu.VMEM((chips, 2 * rows, hidden_units), BF),
+            pltpu.VMEM((chips, 2 * rows, 1), F32),
             pltpu.VMEM((steps * rows, shared_up.shape[1]), BF),
             pltpu.VMEM((steps * rows, width), F32),
             dma((4,)), dma((steps,)), dma((steps,)),
             dma((steps, lines)), dma((steps, lines)), dma((steps, lines)),
             dma((steps, 2 * lines)), dma((steps, chips)),
             dma((steps, chips)), dma((steps, chips)),
-            dma((steps,)), dma((steps,)),
+            dma((steps, chips)), dma((steps, chips)),
             dma((steps, 2 * lines)), dma((steps, 2 * lines)),
             dma((steps, lines)), dma((steps, lines)),
             dma((steps, lines)), dma((steps, lines)),
@@ -486,7 +546,10 @@
             flops=flops, bytes_accessed=4 * 2 * width * hidden_units, transcendentals=0
         ),
         name="fused_layer",
-    )(packed, alive, slot_up, slot_down, shared_up, shared_down)
+    )(
+        hidden_rows, draft_len, expert_ids, replica, route_gain,
+        slot_up, slot_down, shared_up, shared_down,
+    )
 
 
 def slot_gains(lengths, chosen, second, gains, slot_count):

time: 110 us -> 108 us (0.982)
  other arithmetic: 2.39 us -> 0 us
    unnamed x3 -> x4, local copies, waits for them, and re-layouts: 3.18 us -> 5.76 us
where the time goes in v3:
time: 108 us; the launch traced here: 107 us
  Pallas kernels  102 us (94%)
  local copies, waits for them, and re-layouts  5.76 us (5%)
    pallas_call x1, Pallas kernels, fused_layer(): pl.pallas_call(fused, out_shape=jax.ShapeDtypeStruct((steps, rows, width)...  102 us
    unnamed x4, local copies, waits for them, and re-layouts  5.76 us

profile of v3, /device:TPU:1, one launch (start us, length us, event | category | flops | bytes accessed | tf_op | source)
XLA Modules:
  0.0 107.3 jit_solution(5872359771245058430)
XLA Ops:
  0.0 1.4 %copy.10.ids_ref = s32[2,16,8]{2,1,0:T(8,128)} copy(s32[2,16,8]{1,2,0:T(8,128)} %param.11) | data formatting | bytes 2048 | tf_op args[2]
  1.4 1.4 %copy.11.second_ref = s32[2,16,8]{2,1,0:T(8,128)} copy(s32[2,16,8]{1,2,0:T(8,128)} %param.12) | data formatting | bytes 2048 | tf_op args[3]
  2.8 1.4 %copy.12.gain_ref = f32[2,16,8]{2,1,0:T(8,128)} copy(f32[2,16,8]{1,2,0:T(8,128)} %param.13) | data formatting | bytes 2048 | tf_op args[4]
  4.1 101.5 %fused_layer.1 = bf16[2,16,3584]{2,1,0:T(8,128)(2,1)} custom-call(bf16[2,16,3584]{2,1,0:T(8,128)(2,1)} %own_ref.1, s32[2,4]{1,0:T(2,128)} %len_ref.1, s32[2,16,8]{2,1,0:T(8,128)} %copy.10.ids_ref, s32[2,16,8]{2,1,0:T(8,128)} %copy.11.second_ref, f32[2,16,8]{2,1,0:T(8,128)} %copy.12.gain_ref, bf16[1,3584,1024]{2,1,0:T(8,128)(2,1)} %up_hbm.1, ...), custom_call_target="tpu_custom_call" | custom-call | flops 15502147584 | bytes 29360128 | tf_op jit(solution)/shard_map/fused_layer/pallas_call | solution.py:507
  105.7 1.6 %copy.14 = bf16[2,16,3584]{2,1,0:T(8,128)(2,1)} copy(bf16[2,16,3584]{2,1,0:T(8,128)(2,1)} %fused_layer.1) | data formatting | bytes 458752

commit v4 on v3

--- a/solution.py
+++ b/solution.py
@@ -21,10 +21,10 @@
 
 def fused(
     own_ref, len_ref, ids_ref, second_ref, gain_ref, up_hbm, down_hbm, sup_hbm, sdown_hbm,
-    out_ref, x_ref, live_ref, gat, part, swapped, from_f, from_s, from_up, from_dn, from_fin,
+    out_ref, x_ref, live_ref, gat, part, swapped, from_f, from_c, from_s, from_up, from_dn, from_fin,
     up, down, sup, sdown, hid, gain, shid, shout,
     w_sem, swap_s, swap_r, zu_s, zd_s, d1_s, d2_s, ag_r, sib_s, sib_r,
-    x0_s, x0_r, f_s, f_r, s_s, s_r, ru_s, ru_r, rd_s, rd_r, fin_s, fin_r,
+    x0_s, x0_r, f_s, f_r, s_s, s_r, ru_s, ru_r, rd_s, rd_r, fin_s, fin_r, cx_s, c_s, c_r,
 ):
     steps = gat.shape[1]
     chips = gat.shape[2]
@@ -42,10 +42,18 @@
     d2 = y + c * (x - y)
     w1 = 1 + c
     w2 = 2 - c
-    turn = 1 - 2 * (z // (lines // 2))
+    upper = z // 2
+    inner = (z + 1) // 2 == 1
+    turn = 1 - 2 * upper
 
     def chip_of(zz, a, b):
         return zz * 4 + a * w1 + b * w2
+
+    def same(k):
+        return z + k * (4 * upper + 1 - 2 * z)
+
+    def other(k):
+        return 2 + k - upper * (1 + 2 * k)
 
     def order(k):
         return (z + turn * k + lines) % lines
@@ -53,6 +61,8 @@
     sib = chip * 2 + (1 - c)
     above = me + 8
     below = me - 8
+    toward = me + 8 * turn
+    away = me - 8 * turn
     n1 = chip_of(z, 1 - d1, d2) * 2 + c
     n2 = chip_of(z, d1, 1 - d2) * 2 + c
 
@@ -96,18 +106,26 @@
     span = rows // spans
     row_at = lax.broadcasted_iota(jnp.int32, (rows, spans), 0)
     start_at = lax.broadcasted_iota(jnp.int32, (rows, spans), 1) * span
-    lane_at = lax.broadcasted_iota(jnp.int32, (rows, EXTRA), 1)
+    lane_at = lax.broadcasted_iota(jnp.int32, (rows, EXTRA), 1).astype(F32)
+    square = (rows, rows)
+    diagonal = lax.broadcasted_iota(jnp.int32, square, 0) == lax.broadcasted_iota(
+        jnp.int32, square, 1
+    )
     for s in range(steps):
         lens = jnp.minimum(len_ref[pl.ds(s, 1), :], span)
         inside = (row_at >= start_at) & (row_at < start_at + lens)
         alive = jnp.sum(jnp.where(inside, 1.0, 0.0), axis=1, keepdims=True)
         ids = ids_ref[s]
         moved = (ids < replicas) & (second_ref[s] == 1)
-        slot = jnp.where(moved, ids + (slot_count - replicas), ids)
+        slot = jnp.where(moved, ids + (slot_count - replicas), ids).astype(F32)
         weights = gain_ref[s]
         dense = jnp.zeros((rows, EXTRA), F32)
-        for k in range(ids.shape[1]):
-            dense = dense + jnp.where(lane_at == slot[:, k : k + 1], weights[:, k : k + 1], 0.0)
+        for k in range(ids.shape[0]):
+            named = jnp.where(diagonal, slot[k : k + 1, :], 0.0)
+            heavy = jnp.where(diagonal, weights[k : k + 1, :], 0.0)
+            named = jnp.sum(named, axis=1, keepdims=True)
+            heavy = jnp.sum(heavy, axis=1, keepdims=True)
+            dense = dense + jnp.where(lane_at == named, heavy, 0.0)
         dense = dense * alive
         high = dense.astype(BF)
         x_ref[0, s, :, :half] = own_ref[s, :, :half]
@@ -152,7 +170,11 @@
 
     def spread(s, zz):
         go_d1(s, zz).start()
-        go_d2(s, d1, zz).start()
+
+        @pl.when(zz // 2 == upper)
+        def _():
+            go_d2(s, d1, zz).start()
+
         go_sib(s, chip_of(zz, d1, d2)).start()
 
     def ag_own(s):
@@ -196,10 +218,27 @@
         go_d2(s, 1 - d1, zz).start()
         go_sib(s, chip_of(zz, 1 - d1, d2)).start()
 
+    def go_z(s, zz, dev):
+        who = chip_of(zz, d1, 1 - d2)
+        b = block(s, who)
+        return send(b, b, cx_s.at[s, zz], ag_r.at[s, who], dev)
+
     def ag_d2(s, m):
-        a = (d1 + m // lines) % 2
-        who = chip_of(order(m % lines), a, 1 - d2)
+        first_two = 1 - jnp.minimum(m // 2, 1)
+        last_two = m // 6
+        between = 1 - first_two - last_two
+        zz = first_two * same(m) + between * order(m - 2) + last_two * other(m - 6)
+        who = chip_of(zz, d1 + between * (1 - 2 * d1), 1 - d2)
         arrived(s, who)
+
+        @pl.when(inner & (m < 2))
+        def _():
+            go_z(s, zz, toward).start()
+
+        @pl.when(inner & (m >= 6))
+        def _():
+            go_z(s, zz, away).start()
+
         go_sib(s, who).start()
 
     def loop(n, body):
@@ -276,12 +315,53 @@
         i = a * lines + zz
         return send(part.at[c, s, who], from_f.at[s, i], f_s.at[s, i], f_r.at[s, i], n2)
 
-    def rs_f(s, q):
-        a = (1 - d1 + q // lines) % 2
-        zz = order(q % lines)
-        who = chip_of(zz, a, 1 - d2)
-        part[c, s, who] = both_cores(s, who).astype(BF)
-        f_copy(s, a, zz).start()
+    def c_copy(s, zz):
+        who = chip_of(zz, d1, 1 - d2)
+        return send(part.at[c, s, who], from_c.at[s, zz], c_s.at[s, zz], c_r.at[s, zz], toward)
+
+    def with_c(s, zz):
+        c_copy(s, zz).wait_recv()
+        return both_cores(s, chip_of(zz, d1, 1 - d2)) + from_c[s, zz].astype(F32)
+
+    def rs_f(s):
+        @pl.when(jnp.logical_not(inner))
+        def _():
+            for k in range(2):
+                zz = other(k)
+                who = chip_of(zz, d1, 1 - d2)
+                part[c, s, who] = both_cores(s, who).astype(BF)
+                c_copy(s, zz).start()
+
+        def one(q):
+            zz = order(q)
+            who = chip_of(zz, 1 - d1, 1 - d2)
+            part[c, s, who] = both_cores(s, who).astype(BF)
+            f_copy(s, 1 - d1, zz).start()
+
+        loop(lines, one)
+
+    def rs_cross(s):
+        @pl.when(inner)
+        def _():
+            for k in range(2):
+                zz = other(k)
+                part[c, s, chip_of(zz, d1, 1 - d2)] = with_c(s, zz).astype(BF)
+                c_copy(s, zz).start()
+
+    def rs_f_same(s):
+        for k in range(2):
+            zz = same(k)
+            who = chip_of(zz, d1, 1 - d2)
+
+            @pl.when(inner)
+            def _():
+                part[c, s, who] = with_c(s, zz).astype(BF)
+
+            @pl.when(jnp.logical_not(inner))
+            def _():
+                part[c, s, who] = both_cores(s, who).astype(BF)
+
+            f_copy(s, d1, zz).start()
 
     def with_f(s, a, zz):
         f_copy(s, a, zz).wait_recv()
@@ -307,14 +387,14 @@
         return send(part.at[c, s, who], from_dn.at[s, zz], rd_s.at[s, zz], rd_r.at[s, zz], below)
 
     def rs_z(s):
-        def collect(k):
-            zz = order(k)
+        for k in range(lines):
+            near = k < 2
+            zz = same(k) if near else other(k - 2)
             who = chip_of(zz, d1, d2)
-            v = with_f(s, d1, zz)
+            v = with_f(s, d1, zz) if near else both_cores(s, who)
             s_copy(s, zz).wait_recv()
             part[c, s, who] = (v + from_s[s, zz].astype(F32)).astype(BF)
 
-        loop(lines, collect)
         for d in range(lines - 1, 0, -1):
             @pl.when(z + d < lines)
             def _():
@@ -408,7 +488,7 @@
     loop(chunks, lambda j: down_chunk(0, 1 - c, True, j))
     x0_start(0, True)
     loop(chunks, lambda j: down_chunk(0, c, True, j))
-    loop(2 * lines, lambda q: rs_f(0, q))
+    rs_f(0)
 
     def fourth(j):
         down_chunk(0, 1 - c, False, j)
@@ -419,6 +499,7 @@
 
     loop(chunks, fourth)
     x0_start(0, False)
+    rs_cross(0)
 
     def fifth(j):
         down_chunk(0, c, False, j)
@@ -428,6 +509,7 @@
             ag_d2(1, j - late + lines)
 
     loop(chunks, fifth)
+    rs_f_same(0)
     ag_finish(1)
     gains(1)
     loop(hidden_units // 256, lambda i: up_chunk(1, i))
@@ -442,10 +524,12 @@
     loop(chunks, sixth)
     x0_start(1, True)
     loop(chunks, lambda j: down_chunk(1, c, True, j))
-    loop(2 * lines, lambda q: rs_f(1, q))
+    rs_f(1)
     loop(chunks, lambda j: down_chunk(1, 1 - c, False, j))
     x0_start(1, False)
+    rs_cross(1)
     loop(chunks, lambda j: down_chunk(1, c, False, j))
+    rs_f_same(1)
     rs_z(0)
     loop(lines, lambda k: rs_s(1, k))
     rs_own(0)
@@ -460,10 +544,22 @@
 
         def planes(zz):
             go_d1(s, zz).wait_send()
-            go_d2(s, 0, zz).wait_send()
-            go_d2(s, 1, zz).wait_send()
-            f_copy(s, 0, zz).wait_send()
-            f_copy(s, 1, zz).wait_send()
+            go_d2(s, 1 - d1, zz).wait_send()
+            f_copy(s, 1 - d1, zz).wait_send()
+
+            @pl.when(zz // 2 == upper)
+            def _():
+                go_d2(s, d1, zz).wait_send()
+                f_copy(s, d1, zz).wait_send()
+
+            @pl.when(inner)
+            def _():
+                go_z(s, zz, toward).wait_send()
+
+            @pl.when(zz // 2 != upper)
+            def _():
+                c_copy(s, zz).wait_send()
+
             s_copy(s, zz).wait_send()
 
             @pl.when((zz <= z) & (z < lines - 1))
@@ -519,6 +615,7 @@
             pltpu.VMEM((steps, lines, 2, rows, half), BF),
             pltpu.VMEM((steps, lines, 2, rows, half), BF),
             pltpu.VMEM((steps, lines, 2, rows, half), BF),
+            pltpu.VMEM((steps, lines, 2, rows, half), BF),
             pltpu.VMEM((steps, rows, half), BF),
             pltpu.VMEM(slot_up.shape[1:], BF),
             pltpu.VMEM(slot_down.shape[1:], BF),
@@ -538,6 +635,7 @@
             dma((steps, lines)), dma((steps, lines)),
             dma((steps, lines)), dma((steps, lines)),
             dma((steps,)), dma((steps,)),
+            dma((steps, lines)), dma((steps, lines)), dma((steps, lines)),
         ],
         compiler_params=pltpu.CompilerParams(
             collective_id=0, has_side_effects=True, vmem_limit_bytes=62 * 1024 * 1024
@@ -547,8 +645,8 @@
         ),
         name="fused_layer",
     )(
-        hidden_rows, draft_len, expert_ids, replica, route_gain,
-        slot_up, slot_down, shared_up, shared_down,
+        hidden_rows, draft_len, jnp.swapaxes(expert_ids, 1, 2), jnp.swapaxes(replica, 1, 2),
+        jnp.swapaxes(route_gain, 1, 2), slot_up, slot_down, shared_up, shared_down,
     )
 
 

time: 108 us -> 120 us (1.11)
  Pallas kernels: 102 us -> 118 us
  local copies, waits for them, and re-layouts: 5.76 us -> 1.64 us
    pallas_call x1, Pallas kernels: 102 us -> 118 us  [fused_layer(): pl.pallas_call(fused, out_shape=jax.ShapeDtypeStruct((steps, rows, width)...]
    unnamed x4 -> x1, local copies, waits for them, and re-layouts: 5.76 us -> 1.64 us
where the time goes in v4:
time: 120 us
  Pallas kernels  118 us (98%)
  local copies, waits for them, and re-layouts  1.64 us (1%)
    pallas_call x1, Pallas kernels, fused_layer(): pl.pallas_call(fused, out_shape=jax.ShapeDtypeStruct((steps, rows, width)...  118 us

profile of v4, /device:TPU:1, one launch (start us, length us, event | category | flops | bytes accessed | tf_op | source)
XLA Modules:
  0.0 120.0 jit_solution(11270400168542201280)
XLA Ops:
  0.0 118.3 %fused_layer.1 = bf16[2,16,3584]{2,1,0:T(8,128)(2,1)} custom-call(bf16[2,16,3584]{2,1,0:T(8,128)(2,1)} %own_ref.1, s32[2,4]{1,0:T(2,128)} %len_ref.1, s32[2,8,16]{2,1,0:T(8,128)} %bitcast.3, s32[2,8,16]{2,1,0:T(8,128)} %bitcast.4, f32[2,8,16]{2,1,0:T(8,128)} %bitcast.5, bf16[1,3584,1024]{2,1,0:T(8,128)(2,1)} %up_hbm.1, bf16[1,1024,3584]{2,1,0:T(8,128)(2,1)} %down_hbm.1, ...), custom_call_target="tpu_custom_call" | custom-call | flops 15502147584 | bytes 29360128 | tf_op jit(solution)/shard_map/fused_layer/pallas_call | solution.py:603
  118.3 1.6 %copy.11 = bf16[2,16,3584]{2,1,0:T(8,128)(2,1)} copy(bf16[2,16,3584]{2,1,0:T(8,128)(2,1)} %fused_layer.1) | data formatting | bytes 458752

commit v5 on v3

--- a/solution.py
+++ b/solution.py
@@ -96,18 +96,26 @@
     span = rows // spans
     row_at = lax.broadcasted_iota(jnp.int32, (rows, spans), 0)
     start_at = lax.broadcasted_iota(jnp.int32, (rows, spans), 1) * span
-    lane_at = lax.broadcasted_iota(jnp.int32, (rows, EXTRA), 1)
+    lane_at = lax.broadcasted_iota(jnp.int32, (rows, EXTRA), 1).astype(F32)
+    square = (rows, rows)
+    diagonal = lax.broadcasted_iota(jnp.int32, square, 0) == lax.broadcasted_iota(
+        jnp.int32, square, 1
+    )
     for s in range(steps):
         lens = jnp.minimum(len_ref[pl.ds(s, 1), :], span)
         inside = (row_at >= start_at) & (row_at < start_at + lens)
         alive = jnp.sum(jnp.where(inside, 1.0, 0.0), axis=1, keepdims=True)
         ids = ids_ref[s]
         moved = (ids < replicas) & (second_ref[s] == 1)
-        slot = jnp.where(moved, ids + (slot_count - replicas), ids)
+        slot = jnp.where(moved, ids + (slot_count - replicas), ids).astype(F32)
         weights = gain_ref[s]
         dense = jnp.zeros((rows, EXTRA), F32)
-        for k in range(ids.shape[1]):
-            dense = dense + jnp.where(lane_at == slot[:, k : k + 1], weights[:, k : k + 1], 0.0)
+        for k in range(ids.shape[0]):
+            named = jnp.where(diagonal, slot[k : k + 1, :], 0.0)
+            heavy = jnp.where(diagonal, weights[k : k + 1, :], 0.0)
+            named = jnp.sum(named, axis=1, keepdims=True)
+            heavy = jnp.sum(heavy, axis=1, keepdims=True)
+            dense = dense + jnp.where(lane_at == named, heavy, 0.0)
         dense = dense * alive
         high = dense.astype(BF)
         x_ref[0, s, :, :half] = own_ref[s, :, :half]
@@ -166,28 +174,27 @@
         def _():
             go_dn(s, z).start()
 
-        spread(s, z)
-
-    def ag_line(s):
-        for d in range(1, lines):
-            @pl.when(z - d >= 0)
-            def _():
-                arrived(s, chip_of(z - d, d1, d2))
-
-                @pl.when(z < lines - 1)
-                def _():
-                    go_up(s, z - d).start()
-
+    def ag_line(s, d):
+        @pl.when(z - d >= 0)
+        def _():
+            arrived(s, chip_of(z - d, d1, d2))
+
+            @pl.when(z < lines - 1)
+            def _():
+                go_up(s, z - d).start()
+
+            if s == 0:
                 spread(s, z - d)
 
-            @pl.when(z + d < lines)
-            def _():
-                arrived(s, chip_of(z + d, d1, d2))
-
-                @pl.when(z > 0)
-                def _():
-                    go_dn(s, z + d).start()
-
+        @pl.when(z + d < lines)
+        def _():
+            arrived(s, chip_of(z + d, d1, d2))
+
+            @pl.when(z > 0)
+            def _():
+                go_dn(s, z + d).start()
+
+            if s == 0:
                 spread(s, z + d)
 
     def ag_d1(s, k):
@@ -306,7 +313,7 @@
         who = chip_of(zz, d1, d2)
         return send(part.at[c, s, who], from_dn.at[s, zz], rd_s.at[s, zz], rd_r.at[s, zz], below)
 
-    def rs_z(s):
+    def rs_collect(s):
         def collect(k):
             zz = order(k)
             who = chip_of(zz, d1, d2)
@@ -315,32 +322,33 @@
             part[c, s, who] = (v + from_s[s, zz].astype(F32)).astype(BF)
 
         loop(lines, collect)
-        for d in range(lines - 1, 0, -1):
-            @pl.when(z + d < lines)
-            def _():
-                zz = z + d
-                who = chip_of(zz, d1, d2)
-
-                @pl.when(z > 0)
-                def _():
-                    up_copy(s, zz).wait_recv()
-                    v = part[c, s, who].astype(F32) + from_up[s, zz].astype(F32)
-                    part[c, s, who] = v.astype(BF)
-
-                up_copy(s, zz).start()
-
-            @pl.when(z - d >= 0)
-            def _():
-                zz = z - d
-                who = chip_of(zz, d1, d2)
-
-                @pl.when(z < lines - 1)
-                def _():
-                    dn_copy(s, zz).wait_recv()
-                    v = part[c, s, who].astype(F32) + from_dn[s, zz].astype(F32)
-                    part[c, s, who] = v.astype(BF)
-
-                dn_copy(s, zz).start()
+
+    def rs_hop(s, d):
+        @pl.when(z + d < lines)
+        def _():
+            zz = z + d
+            who = chip_of(zz, d1, d2)
+
+            @pl.when(z > 0)
+            def _():
+                up_copy(s, zz).wait_recv()
+                v = part[c, s, who].astype(F32) + from_up[s, zz].astype(F32)
+                part[c, s, who] = v.astype(BF)
+
+            up_copy(s, zz).start()
+
+        @pl.when(z - d >= 0)
+        def _():
+            zz = z - d
+            who = chip_of(zz, d1, d2)
+
+            @pl.when(z < lines - 1)
+            def _():
+                dn_copy(s, zz).wait_recv()
+                v = part[c, s, who].astype(F32) + from_dn[s, zz].astype(F32)
+                part[c, s, who] = v.astype(BF)
+
+            dn_copy(s, zz).start()
 
     def fin(s):
         return send(part.at[c, s, chip, 1 - c], from_fin.at[s], fin_s.at[s], fin_r.at[s], sib)
@@ -375,16 +383,24 @@
         gat[c, s, chip, c] = x_ref[c, s]
         swap(s).start()
     ag_own(0)
-    ag_line(0)
+    spread(0, z)
+    ag_own(1)
+    for d in range(1, lines):
+        ag_line(0, d)
+        ag_line(1, d)
+        if d < lines - 1:
+            ag_d1(0, d - 1)
     loads[0].wait()
 
     def first(k):
-        ag_d1(0, k)
         shared_up_chunk(k)
 
+        @pl.when(k < 2)
+        def _():
+            ag_d1(0, k + lines - 2)
+
     loop(lines, first)
-    ag_own(1)
-    ag_line(1)
+    loop(lines, lambda k: spread(1, order(k)))
     loads[1].wait()
 
     def second(m):
@@ -443,13 +459,19 @@
     x0_start(1, True)
     loop(chunks, lambda j: down_chunk(1, c, True, j))
     loop(2 * lines, lambda q: rs_f(1, q))
+    rs_collect(0)
+    rs_hop(0, 3)
     loop(chunks, lambda j: down_chunk(1, 1 - c, False, j))
     x0_start(1, False)
+    rs_hop(0, 2)
     loop(chunks, lambda j: down_chunk(1, c, False, j))
-    rs_z(0)
+    rs_hop(0, 1)
     loop(lines, lambda k: rs_s(1, k))
     rs_own(0)
-    rs_z(1)
+    rs_collect(1)
+    rs_hop(1, 3)
+    rs_hop(1, 2)
+    rs_hop(1, 1)
     write(0)
     rs_own(1)
     write(1)
@@ -547,8 +569,8 @@
         ),
         name="fused_layer",
     )(
-        hidden_rows, draft_len, expert_ids, replica, route_gain,
-        slot_up, slot_down, shared_up, shared_down,
+        hidden_rows, draft_len, jnp.swapaxes(expert_ids, 1, 2), jnp.swapaxes(replica, 1, 2),
+        jnp.swapaxes(route_gain, 1, 2), slot_up, slot_down, shared_up, shared_down,
     )
 
 

time: 108 us -> 99.5 us (0.921)
  Pallas kernels: 102 us -> 97.7 us
  local copies, waits for them, and re-layouts: 5.76 us -> 1.64 us
    unnamed x4 -> x1, local copies, waits for them, and re-layouts: 5.76 us -> 1.64 us
    pallas_call x1, Pallas kernels: 102 us -> 97.7 us  [fused_layer(): pl.pallas_call(fused, out_shape=jax.ShapeDtypeStruct((steps, rows, width)...]
where the time goes in v5:
time: 99.5 us; the launch traced here: 99.3 us
  Pallas kernels  97.7 us (98%)
  local copies, waits for them, and re-layouts  1.64 us (2%)
    pallas_call x1, Pallas kernels, fused_layer(): pl.pallas_call(fused, out_shape=jax.ShapeDtypeStruct((steps, rows, width)...  97.7 us

profile of v5, /device:TPU:1, one launch (start us, length us, event | category | flops | bytes accessed | tf_op | source)
XLA Modules:
  0.0 99.3 jit_solution(11671294287265179127)
XLA Ops:
  0.0 97.7 %fused_layer.1 = bf16[2,16,3584]{2,1,0:T(8,128)(2,1)} custom-call(bf16[2,16,3584]{2,1,0:T(8,128)(2,1)} %own_ref.1, s32[2,4]{1,0:T(2,128)} %len_ref.1, s32[2,8,16]{2,1,0:T(8,128)} %bitcast.3, s32[2,8,16]{2,1,0:T(8,128)} %bitcast.4, f32[2,8,16]{2,1,0:T(8,128)} %bitcast.5, bf16[1,3584,1024]{2,1,0:T(8,128)(2,1)} %up_hbm.1, bf16[1,1024,3584]{2,1,0:T(8,128)(2,1)} %down_hbm.1, ...), custom_call_target="tpu_custom_call" | custom-call | flops 15502147584 | bytes 29360128 | tf_op jit(solution)/shard_map/fused_layer/pallas_call | solution.py:529
  97.7 1.6 %copy.11 = bf16[2,16,3584]{2,1,0:T(8,128)(2,1)} copy(bf16[2,16,3584]{2,1,0:T(8,128)(2,1)} %fused_layer.1) | data formatting | bytes 458752

commit v6 on v5

--- a/solution.py
+++ b/solution.py
@@ -76,9 +76,9 @@
         )
     ]
     loads[0].start()
-    loads[1].start()
     loads[2].start()
     loads[3].start()
+    loads[1].start()
     for dev in (sib, n1, n2):
         greet(dev)
 
@@ -401,14 +401,7 @@
 
     loop(lines, first)
     loop(lines, lambda k: spread(1, order(k)))
-    loads[1].wait()
-
-    def second(m):
-        ag_d2(0, m)
-        shared_down_chunk(m)
-
-    loop(2 * lines - 1, second)
-    ag_d2(0, 2 * lines - 1)
+    loop(2 * lines, lambda m: ag_d2(0, m))
     ag_finish(0)
     loads[2].wait()
     gains(0)
@@ -467,10 +460,14 @@
     loop(chunks, lambda j: down_chunk(1, c, False, j))
     rs_hop(0, 1)
     loop(lines, lambda k: rs_s(1, k))
+    loads[1].wait()
+    loop(3, shared_down_chunk)
     rs_own(0)
     rs_collect(1)
     rs_hop(1, 3)
+    loop(2, lambda j: shared_down_chunk(3 + j))
     rs_hop(1, 2)
+    loop(2, lambda j: shared_down_chunk(5 + j))
     rs_hop(1, 1)
     write(0)
     rs_own(1)

time: 99.5 us -> 99.5 us (level)
  no operation moved by 1% of the time
where the time goes in v6:
time: 99.5 us; the launch traced here: 99.3 us
  Pallas kernels  97.7 us (98%)
  local copies, waits for them, and re-layouts  1.64 us (2%)
    pallas_call x1, Pallas kernels, fused_layer(): pl.pallas_call(fused, out_shape=jax.ShapeDtypeStruct((steps, rows, width)...  97.7 us

profile of v6, /device:TPU:1, one launch (start us, length us, event | category | flops | bytes accessed | tf_op | source)
XLA Modules:
  0.0 99.3 jit_solution(2475973287770242209)
XLA Ops:
  0.0 97.7 %fused_layer.1 = bf16[2,16,3584]{2,1,0:T(8,128)(2,1)} custom-call(bf16[2,16,3584]{2,1,0:T(8,128)(2,1)} %own_ref.1, s32[2,4]{1,0:T(2,128)} %len_ref.1, s32[2,8,16]{2,1,0:T(8,128)} %bitcast.3, s32[2,8,16]{2,1,0:T(8,128)} %bitcast.4, f32[2,8,16]{2,1,0:T(8,128)} %bitcast.5, bf16[1,3584,1024]{2,1,0:T(8,128)(2,1)} %up_hbm.1, bf16[1,1024,3584]{2,1,0:T(8,128)(2,1)} %down_hbm.1, ...), custom_call_target="tpu_custom_call" | custom-call | flops 15502147584 | bytes 29360128 | tf_op jit(solution)/shard_map/fused_layer/pallas_call | solution.py:526
  97.7 1.6 %copy.11 = bf16[2,16,3584]{2,1,0:T(8,128)(2,1)} copy(bf16[2,16,3584]{2,1,0:T(8,128)(2,1)} %fused_layer.1) | data formatting | bytes 458752
